TPU v7x, 256 devices: a whole 4x4x8 slice. The times are simulated.
256 devices in a mesh: blk: 32 (over z_hi, x, y), dp: 8 (over z_lo, core).
Axes of the slice: x: 4, y: 4, z: 8 (z_hi: 2, z_lo: 4; z = z_hi * 4 + z_lo), core: 2. Of those that a mesh axis runs over, the one named last changes fastest.
Arguments:
- image_embed: bfloat16 [49152, 1024], P(('blk', 'dp')), may hold values from -0.19921875 to 0.19921875
- text_embed: bfloat16 [49152, 1024], P(('blk', 'dp')), may hold values from -0.19921875 to 0.19921875
- log_logit_scale: float32 [1], replicated, may hold values from 1.6 to 3
- logit_bias: float32 [1], replicated, may hold values from -7 to -5
Outputs:
- image_gradient: bfloat16 [49152, 1024], P(('blk', 'dp'))
- text_gradient: bfloat16 [49152, 1024], P(('blk', 'dp'))
- log_scale_gradient: float32 [1], replicated
- grad_bias: float32 [1], replicated
- loss: float32 [1], replicated
All inputs are finite; a program needn't handle non-finite values.
Results may differ from a plain program's by a relative error of at most 0.001.
The roundings to bfloat16 on the way count: a program that leaves them out, or rounds other values in their place, can miss the bound.
Values may be sent and summed in bfloat16 or wider, within the bound.
A program may use at most 128 MiB of HBM per device.

v0:
```python
import jax
import jax.numpy as jnp
from jax import lax
from jax.sharding import PartitionSpec as P

EPS = 1e-06


def unit_rows(raw):
    widened = raw.astype(jnp.float32)
    inverse = lax.rsqrt(jnp.sum(widened * widened, axis=1, keepdims=True) + EPS)
    unit_vec = widened * inverse
    return (unit_vec, inverse, unit_vec.astype(jnp.bfloat16))


def unscaled_gradient(unit_vec, inverse, scaled):
    along = jnp.sum(unit_vec * scaled, axis=1, keepdims=True)
    return ((scaled - unit_vec * along) * inverse).astype(jnp.bfloat16)


def pairwise_losses(local_portion, remote_portion, logit_scale, shift_bias, local_leading):
    cosine_matrix = lax.dot_general(
        local_portion, remote_portion, (((1,), (1,)), ((), ())), preferred_element_type=jnp.float32
    )
    logit_matrix = logit_scale * cosine_matrix + shift_bias
    row_ids = local_leading + lax.broadcasted_iota(jnp.int32, cosine_matrix.shape, 0)
    col_ids = lax.broadcasted_iota(jnp.int32, cosine_matrix.shape, 1)
    pair_sign = jnp.where(row_ids == col_ids, 1.0, -1.0).astype(jnp.float32)
    pair_loss = jax.nn.softplus(-pair_sign * logit_matrix)
    pair_coef = -pair_sign * jax.nn.sigmoid(-pair_sign * logit_matrix)
    return (cosine_matrix, pair_coef, jnp.sum(pair_loss))


def per_device(image_embed, text_embed, log_logit_scale, logit_bias):
    own_rows = image_embed.shape[0]
    cycle_size = lax.axis_size("blk")
    groups = lax.axis_size("dp")
    local_leading = lax.axis_index("blk") * own_rows
    logit_scale = jnp.exp(log_logit_scale[0])
    shift_bias = logit_bias[0]
    image_normalized_rows, image_inverse_norm, image_portion = unit_rows(image_embed)
    text_normalized_rows, text_inverse_norm, text_half = unit_rows(text_embed)
    rows_per_block = lax.all_gather(text_half, "blk", axis=0, tiled=True)
    cosine_matrix, pair_coef, loss_part = pairwise_losses(
        image_portion, rows_per_block, logit_scale, shift_bias, local_leading
    )
    coef_half = pair_coef.astype(jnp.bfloat16)
    grad_sum = jnp.dot(coef_half, rows_per_block, preferred_element_type=jnp.float32)
    folded = (
        grad_sum,
        coef_half,
        loss_part,
        jnp.sum(pair_coef * cosine_matrix),
        jnp.sum(pair_coef),
    )
    image_partial, coef_all, loss_sum, temp_sum, bias_sum = folded
    text_partial = lax.psum_scatter(
        lax.dot_general(
            coef_all, image_portion, (((0,), (0,)), ((), ())), preferred_element_type=jnp.float32
        ),
        "blk",
        scatter_dimension=0,
        tiled=True,
    )
    grand_totals = lax.psum((loss_sum, temp_sum, bias_sum), ("blk", "dp"))
    rows_in_batch = own_rows * cycle_size * groups
    image_gradient = unscaled_gradient(
        image_normalized_rows, image_inverse_norm, logit_scale * image_partial
    )
    text_gradient = unscaled_gradient(
        text_normalized_rows, text_inverse_norm, logit_scale * text_partial
    )
    loss = (grand_totals[0] / rows_in_batch).reshape(1)
    log_scale_gradient = (logit_scale * grand_totals[1] / rows_in_batch).reshape(1)
    grad_bias = (grand_totals[2] / rows_in_batch).reshape(1)
    return (image_gradient, text_gradient, log_scale_gradient, grad_bias, loss)


def solution(mesh):
    placed = (P(("blk", "dp"), None), P(("blk", "dp"), None), P(), P())
    return jax.shard_map(
        per_device,
        mesh=mesh,
        in_specs=placed,
        out_specs=(P(("blk", "dp"), None), P(("blk", "dp"), None), P(), P(), P()),
        check_vma=False,
    )
```

profile of v0, /device:TPU:33, one launch (start us, length us, event | category | flops | bytes accessed | tf_op | source)
XLA Modules:
  0.0 715.3 jit_solution(10629701139418682687)
XLA Ops:
  7.2 0.0 all-gather.2.cloned.1.call-start
  7.2 1.2 fusion.19
  8.4 1.9 fusion.6
  10.3 0.0 all-gather.2.cloned.1.call-update
  10.3 0.0 reduce-scatter.2.cloned.1.call-start
  11.7 1.2 fusion.14
  12.8 199.1 %all-gather.2.cloned.1.call-done = bf16[6144,1024]{1,0:T(8,128)(2,1)} async-done(((bf16[192,1024]{1,0:T(8,128)(2,1)}), bf16[6144,1024]{1,0:T(8,128)(2,1)}) %all-gather.2.cloned.1.call-update) | async-done | bytes 12582928 | tf_op jit(solution)/shard_map/all_gather | solution.py:43
  211.9 0.0 copy-start.1
  211.9 13.6 %fusion = (f32[]{:T(128)}, f32[]{:T(128)}, f32[]{:T(128)}, f32[192,6144]{1,0:T(8,128)S(1)}) fusion(f32[]{:T(128)} %bitcast.8, f32[]{:T(128)} %bitcast, s32[192]{0:T(256)S(1)} %iota_add_fusion, bf16[6144,1024]{1,0:T(8,128)(2,1)} %all-gather.2.cloned.1.call-done, bf16[192,1024]{1,0:T(8,128)(2,1)} %param.4, f32[192]{0:T(256)S(1)} %add_rsqrt_fusion.1), kind=kOutput, calls=%fused_computation.1 | convolution fusion | flops 2440101888 | bytes 17696276 | tf_op jit(solution)/shard_map/dot_general | solution.py:22
  225.6 0.0 copy-start.2
  225.6 2.2 copy-done.2
  227.7 0.0 copy-done.1
  227.7 10.7 %fusion.1 = f32[6144,1024]{1,0:T(8,128)} fusion(bf16[192,1024]{1,0:T(8,128)(2,1)S(1)} %copy-done.1, f32[192]{0:T(256)S(1)} %add_rsqrt_fusion.1, f32[192,6144]{1,0:T(8,128)S(1)} %get-tuple-element.13, f32[]{:T(128)} %bitcast.9, f32[]{:T(128)} %bitcast, s32[192]{0:T(256)S(1)} %iota_add_fusion), kind=kOutput, calls=%fused_computation.8 | convolution fusion | flops 2429485056 | bytes 30279176 | tf_op jit(solution)/shard_map/dot_general | solution.py:58
  238.4 0.0 reduce-scatter.2.cloned.1.call-update
  238.4 89.8 %all-reduce = (f32[]{:T(128)}, f32[]{:T(128)}, f32[]{:T(128)}) all-reduce(f32[]{:T(128)} %get-tuple-element.7, f32[]{:T(128)} %get-tuple-element.6, f32[]{:T(128)} %get-tuple-element.5), channel_id=1, replica_groups=mesh['blk'=32,'dp'=8] {'blk','dp'}, use_global_device_ids=true, to_apply=%region_6.7 | all-reduce | flops 3 | bytes 24 | tf_op jit(solution)/shard_map/psum | solution.py:65
  330.2 0.0 copy-start
  330.2 10.2 %fusion.10 = (f32[192]{0:T(256)S(1)}, f32[192,1024]{1,0:T(8,128)S(1)}) fusion(bf16[192,1024]{1,0:T(8,128)(2,1)S(1)} %copy-done.1, f32[192]{0:T(256)S(1)} %add_rsqrt_fusion.1, bf16[6144,1024]{1,0:T(8,128)(2,1)} %all-gather.2.cloned.1.call-done, f32[]{:T(128)} %bitcast.7, f32[192,6144]{1,0:T(8,128)} %copy-done.2, f32[]{:T(128)} %bitcast, s32[192]{0:T(256)S(1)} %iota_add_fusion), kind=kOutput, calls=%fused_computation.21 | convolution fusion | flops 2429878016 | bytes 18483464 | tf_op jit(solution)/shard_map/dot_general | solution.py:48
  340.4 1.0 fusion.13
  341.4 360.2 %reduce-scatter.2.cloned.1.call-done = f32[192,1024]{1,0:T(8,128)} async-done(((f32[6144,1024]{1,0:T(8,128)}), f32[192,1024]{1,0:T(8,128)}) %reduce-scatter.2.cloned.1.call-update) | async-done | bytes 786448 | tf_op jit(solution)/shard_map/reduce_scatter | solution.py:57
  701.6 0.0 copy-done
  701.6 1.4 fusion.15
  703.0 2.1 fusion.18
  (3 shorter events, 0.0 us)
Async XLA Ops:
  7.2 204.7 %all-gather.2.cloned.1.call-start = ((), (), s32[]{:S(2)}) async-start(), calls=%async_computation.1 | async-start | bytes 12976128 | tf_op jit(solution)/shard_map/all_gather | solution.py:43
  10.3 691.3 %reduce-scatter.2.cloned.1.call-start = ((), (), s32[]{:S(2)}) async-start(), calls=%async_computation.2 | async-start | bytes 25952256 | tf_op jit(solution)/shard_map/reduce_scatter | solution.py:57
  211.9 15.8 %copy-start.1 = (bf16[192,1024]{1,0:T(8,128)(2,1)S(1)}, bf16[192,1024]{1,0:T(8,128)(2,1)}, u32[]{:S(2)}) copy-start(bf16[192,1024]{1,0:T(8,128)(2,1)} %param.4) | copy-start | bytes 1179652
  225.6 2.2 copy-start.2
  330.2 371.4 %copy-start = (bf16[192,1024]{1,0:T(8,128)(2,1)S(1)}, bf16[192,1024]{1,0:T(8,128)(2,1)}, u32[]{:S(2)}) copy-start(bf16[192,1024]{1,0:T(8,128)(2,1)} %param.5) | copy-start | bytes 1179652
Sparse Core Ops, SparseCore 0:
  12.0 199.8 all-gather.1
  238.6 462.9 reduce-scatter.1
where the time goes:
time: 718 us; the launch traced here: 715 us
  waiting for transfers between devices  559 us (78%)
  blocking collectives  89.8 us (13%)
  matrix products  34.5 us (5%)
  between operations  20.7 us (3%)
  other arithmetic  8.68 us (1%)
    reduce_scatter x1, waiting for transfers between devices, per_device(): lax.psum_scatter(lax.dot_general(coef_all, image_portion, (((0,), (0,)),...  360 us
    all_gather x1, waiting for transfers between devices, per_device(): rows_per_block = lax.all_gather(text_half, 'blk', axis=0, tiled=True)  199 us
    psum x1, blocking collectives, per_device(): grand_totals = lax.psum((loss_sum, temp_sum, bias_sum), ('blk', 'dp'))  89.8 us
  transfers between devices with their start and end apart: 2, of which 2 were waited for; matrix products, arithmetic and copies ran while one was open for 2% of the time, Pallas kernels for 0%

commit v1 on v0

v1 whole, which is shorter than its diff:
```python
import functools

import jax
import jax.numpy as jnp
from jax import lax
from jax.experimental import pallas as pl
from jax.experimental.pallas import tpu as pltpu
from jax.sharding import PartitionSpec as P

EPS = 1e-06
MESH = pl.DeviceIdType.MESH
SIDE = 4
TILE = 256

Z_IN_T, Z_IN_I = 0, 1
AG_T, AG_I = 2, 5
CORE_T, CORE_I = 8, 12
RS_T, RS_I = 16, 19
Z_OUT_T, Z_OUT_I = 22, 23
ST_X, ST_Y, ST_C, ST_L, ST_P = 24, 27, 30, 31, 34
COPIES = 35


def kernel(
    pairs, log_scale_ref, bias_ref, img_ref, txt_ref,
    out_img, out_txt, out_scale, out_bias, out_loss,
    raw, texts, images, coef_own, coef_other, grad_img, grad_txt, recv_img, recv_txt,
    final, acc, st_x, st_y, st_c, st_l, st_p, send_sem, recv_sem,
):
    rows, width = img_ref.shape
    half = SIDE * rows
    blk, dp = lax.axis_index("blk"), lax.axis_index("dp")
    zh, x, y = blk // (SIDE * SIDE), (blk // SIDE) % SIDE, blk % SIDE
    zl, core = dp // 2, dp % 2
    native = core == zh

    def device(dx=0, dy=0, dl=0, other_core=False, other_plane=False):
        h = 1 - zh if other_plane else zh
        c = 1 - core if other_core else core
        return {
            "blk": (h * SIDE + (x + dx) % SIDE) * SIDE + (y + dy) % SIDE,
            "dp": ((zl + dl) % SIDE) * 2 + c,
        }

    along_x = [device(dx=d) for d in (1, 2, 3)]
    along_y = [device(dy=d) for d in (1, 2, 3)]
    along_l = [device(dl=d) for d in (1, 2, 3)]
    sibling = device(other_core=True)
    partner = device(other_core=True, other_plane=True)

    def copy(number, src, dst, where):
        return pltpu.make_async_remote_copy(
            src_ref=src, dst_ref=dst, send_sem=send_sem.at[number], recv_sem=recv_sem.at[number],
            device_id=where, device_id_type=MESH,
        )

    def slot(buffer, index):
        return buffer.at[pl.ds(index * rows, rows)]

    def z_in(number):
        src = (txt_ref, img_ref)[number - Z_IN_T]
        return copy(number, src, raw.at[number - Z_IN_T], partner)

    def gather(base, d):
        buffer, line = (texts, along_x) if base == AG_T else (images, along_y)
        return copy(base + d - 1, slot(buffer, 0), slot(buffer, SIDE - d), line[d - 1])

    def to_core(base, index):
        buffer = texts if base == CORE_T else images
        return copy(base + index, slot(buffer, index), slot(buffer, SIDE + index), sibling)

    def reduce(base, d):
        grad, recv, line = (grad_txt, recv_txt, along_x) if base == RS_T else (grad_img, recv_img, along_y)
        return copy(base + d - 1, slot(grad, d), recv.at[d - 1], line[d - 1])

    def z_out(number):
        which = number - Z_OUT_T
        return copy(number, final.at[which], (out_txt, out_img)[which], partner)

    barrier = pltpu.get_barrier_semaphore()
    everyone = along_x + along_y + along_l + [sibling, partner]
    for other in everyone:
        pl.semaphore_signal(barrier, inc=1, device_id=other, device_id_type=MESH)
    pl.semaphore_wait(barrier, len(everyone))

    def normalize(which, buffer):
        def body(i, _):
            at = pl.ds(pl.multiple_of(i * 16, 16), 16)
            wide = raw[which, at, :].astype(jnp.float32)
            inverse = lax.rsqrt(jnp.sum(wide * wide, axis=1, keepdims=True) + EPS)
            buffer[at, :] = (wide * inverse).astype(jnp.bfloat16)
            return 0

        lax.fori_loop(0, rows // 16, body, 0)

    def share(which, buffer, ag, to):
        normalize(which, buffer)
        for d in (1, 3, 2):
            gather(ag, d).start()
        to_core(to, 0).start()

    def forward(ag, to):
        for d in (1, 3, 2):
            gather(ag, d).wait_recv()
            to_core(to, SIDE - d).start()

    acc[...] = jnp.zeros_like(acc)

    @pl.when(jnp.logical_not(native))
    def _():
        z_in(Z_IN_T).start()
        z_in(Z_IN_I).start()
        z_in(Z_IN_T).wait_recv()

    @pl.when(native)
    def _():
        raw[0] = txt_ref[...]
        raw[1] = img_ref[...]

    scale = jnp.exp(jnp.full((1, TILE), log_scale_ref[0], jnp.float32))
    bias = jnp.full((1, TILE), bias_ref[0], jnp.float32)

    share(0, texts, AG_T, CORE_T)

    @pl.when(native)
    def _():
        share(1, images, AG_I, CORE_I)

    forward(AG_T, CORE_T)
    for index in range(SIDE):
        to_core(CORE_T, index).wait_recv()

    def cosines(left, right):
        return lax.dot_general(left, right, (((1,), (1,)), ((), ())), preferred_element_type=jnp.float32)

    def other_part():
        for index in range(SIDE):
            to_core(CORE_I, index).wait_recv()
        tiles = half // TILE

        def body(step, _):
            i, j = step // tiles, step % tiles
            left = images[pl.ds(pl.multiple_of(half + i * TILE, TILE), TILE), :]
            right = texts[pl.ds(pl.multiple_of(j * TILE, TILE), TILE), :]
            grown = jnp.exp(scale * cosines(left, right) + bias)
            coef_other[pl.ds(pl.multiple_of(i * TILE, TILE), TILE), pl.ds(pl.multiple_of(j * TILE, TILE), TILE)] = (
                grown / (1.0 + grown)
            ).astype(jnp.bfloat16)
            return 0

        lax.fori_loop(0, tiles * tiles, body, 0)

    @pl.when(jnp.logical_not(native))
    def _():
        other_part()
        z_in(Z_IN_I).wait_recv()
        share(1, images, AG_I, CORE_I)

    def own_tile(index, j, diagonal):
        left = images[pl.ds(index * rows, rows), :]
        right = texts[pl.ds(pl.multiple_of(j * TILE, TILE), TILE), :]
        cosine = cosines(left, right)
        logit = scale * cosine + bias
        grown = jnp.exp(logit)
        more = 1.0 + grown
        inverse = 1.0 / more
        coef = grown * inverse
        loss = jnp.log(more)
        if diagonal:
            same = lax.broadcasted_iota(jnp.int32, cosine.shape, 0) == lax.broadcasted_iota(jnp.int32, cosine.shape, 1)
            coef = jnp.where(same, -inverse, coef)
            loss = jnp.where(same, loss - logit, loss)
        coef_own[pl.ds(index * rows, rows), pl.ds(pl.multiple_of(j * TILE, TILE), TILE)] = coef.astype(jnp.bfloat16)
        for k, term in enumerate((loss, coef * cosine, coef)):
            acc[k] += jnp.sum(term.reshape(rows // 8, 8, TILE), axis=0)

    def image_slot(index):
        start = 0
        if index == 0:
            own_tile(0, 0, True)
            start = 1

        def tile(j, _):
            own_tile(index, j, False)
            return 0

        lax.fori_loop(start, 2 * half // TILE, tile, 0)

        def column(n, _):
            at = pl.ds(pl.multiple_of(n * TILE, TILE), TILE)
            grad_img[pl.ds(index * rows, rows), at] = jnp.dot(
                coef_own[pl.ds(index * rows, rows), :], texts[:, at], preferred_element_type=jnp.float32
            )
            return 0

        lax.fori_loop(0, width // TILE, column, 0)

    image_slot(0)
    for d in (1, 3, 2):
        gather(AG_I, d).wait_recv()
        to_core(CORE_I, SIDE - d).start()
        image_slot(SIDE - d)
        reduce(RS_I, SIDE - d).start()

    @pl.when(native)
    def _():
        other_part()

    def sums_start(base, buffer, mine, line):
        for d in range(1, len(line) + 1):
            copy(base + d - 1, buffer.at[mine], buffer.at[mine], line[d - 1]).start()

    def sums_finish(base, buffer, mine, line):
        for d in range(1, len(line) + 1):
            copy(base + d - 1, buffer.at[mine], buffer.at[mine], line[d - 1]).wait_recv()
        return functools.reduce(lambda a, b: a + b, [buffer[i] for i in range(len(line) + 1)])

    stages = (
        (ST_X, st_x, x, along_x),
        (ST_Y, st_y, y, along_y),
        (ST_C, st_c, core, [sibling]),
        (ST_L, st_l, zl, along_l),
        (ST_P, st_p, zh, [partner]),
    )
    folded = acc[:, :, :128] + acc[:, :, 128:]
    st_x[x] = folded.reshape(24, 128)
    sums_start(*stages[0])

    def text_tile(jt):
        at_rows = pl.ds(jt * TILE, TILE)

        def column(n, _):
            at = pl.ds(pl.multiple_of(n * TILE, TILE), TILE)
            over_rows = (((0,), (0,)), ((), ()))
            grad_txt[at_rows, at] = lax.dot_general(
                coef_own[:, at_rows], images[:half, at], over_rows, preferred_element_type=jnp.float32
            ) + lax.dot_general(
                coef_other[:, at_rows], images[half:, at], over_rows, preferred_element_type=jnp.float32
            )
            return 0

        lax.fori_loop(0, width // TILE, column, 0)

    text_tile(1)
    text_tile(2)
    reduce(RS_T, 2).start()
    reduce(RS_T, 3).start()
    text_tile(0)
    reduce(RS_T, 1).start()

    for this, after in zip(stages[:-1], stages[1:]):
        after[1][after[2]] = sums_finish(*this)
        sums_start(*after)
    totals = sums_finish(*stages[-1])
    loss_sum, temp_sum, bias_sum = (
        jnp.sum(jnp.sum(totals[8 * k : 8 * k + 8], axis=0, keepdims=True), axis=1, keepdims=True) for k in range(3)
    )
    out_loss[0] = (loss_sum / pairs)[0, 0]
    out_scale[0] = (scale[:, :1] * temp_sum / pairs)[0, 0]
    out_bias[0] = (bias_sum / pairs)[0, 0]

    def finish(which, grad, recv):
        def body(i, _):
            at = pl.ds(pl.multiple_of(i * 16, 16), 16)
            wide = raw[which, at, :].astype(jnp.float32)
            inverse = lax.rsqrt(jnp.sum(wide * wide, axis=1, keepdims=True) + EPS)
            unit = wide * inverse
            scaled = scale[:, :1] * (grad[at, :] + recv[0, at, :] + recv[1, at, :] + recv[2, at, :])
            along = jnp.sum(unit * scaled, axis=1, keepdims=True)
            final[which, at, :] = ((scaled - unit * along) * inverse).astype(jnp.bfloat16)
            return 0

        lax.fori_loop(0, rows // 16, body, 0)

    for which, rs, grad, recv, out, number in (
        (1, RS_I, grad_img, recv_img, out_img, Z_OUT_I),
        (0, RS_T, grad_txt, recv_txt, out_txt, Z_OUT_T),
    ):
        for d in (1, 2, 3):
            reduce(rs, d).wait_recv()
        finish(which, grad, recv)

        @pl.when(native)
        def _():
            out[...] = final[which]

        @pl.when(jnp.logical_not(native))
        def _():
            z_out(number).start()

    for d in (1, 2, 3):
        gather(AG_T, d).wait_send()
        gather(AG_I, d).wait_send()
        reduce(RS_T, d).wait_send()
        reduce(RS_I, d).wait_send()
    for index in range(SIDE):
        to_core(CORE_T, index).wait_send()
        to_core(CORE_I, index).wait_send()
    for base, buffer, mine, line in stages:
        for d in range(1, len(line) + 1):
            copy(base + d - 1, buffer.at[mine], buffer.at[mine], line[d - 1]).wait_send()

    @pl.when(jnp.logical_not(native))
    def _():
        z_in(Z_IN_T).wait_send()
        z_in(Z_IN_I).wait_send()
        z_out(Z_OUT_I).wait()
        z_out(Z_OUT_T).wait()


def per_device(image_embed, text_embed, log_logit_scale, logit_bias):
    rows, width = image_embed.shape
    half = SIDE * rows
    pairs = rows * lax.axis_size("blk") * lax.axis_size("dp")
    vmem, smem = pl.BlockSpec(memory_space=pltpu.VMEM), pl.BlockSpec(memory_space=pltpu.SMEM)
    one = jax.ShapeDtypeStruct((1,), jnp.float32)
    like = jax.ShapeDtypeStruct((rows, width), jnp.bfloat16)
    bf16, f32 = jnp.bfloat16, jnp.float32
    image_gradient, text_gradient, scale_gradient, bias_gradient, loss = pl.pallas_call(
        functools.partial(kernel, pairs),
        out_shape=(like, like, one, one, one),
        in_specs=[smem, smem, vmem, vmem],
        out_specs=(vmem, vmem, smem, smem, smem),
        scratch_shapes=[
            pltpu.VMEM((2, rows, width), bf16),
            pltpu.VMEM((2 * half, width), bf16),
            pltpu.VMEM((2 * half, width), bf16),
            pltpu.VMEM((half, 2 * half), bf16),
            pltpu.VMEM((half, half), bf16),
            pltpu.VMEM((half, width), f32),
            pltpu.VMEM((half, width), f32),
            pltpu.VMEM((3, rows, width), f32),
            pltpu.VMEM((3, rows, width), f32),
            pltpu.VMEM((2, rows, width), bf16),
            pltpu.VMEM((3, 8, TILE), f32),
            pltpu.VMEM((4, 24, 128), f32),
            pltpu.VMEM((4, 24, 128), f32),
            pltpu.VMEM((2, 24, 128), f32),
            pltpu.VMEM((4, 24, 128), f32),
            pltpu.VMEM((2, 24, 128), f32),
            pltpu.SemaphoreType.DMA((COPIES,)),
            pltpu.SemaphoreType.DMA((COPIES,)),
        ],
        name="contrastive_step",
        compiler_params=pltpu.CompilerParams(
            collective_id=0, has_side_effects=True, vmem_limit_bytes=48 * 2**20
        ),
    )(log_logit_scale, logit_bias, image_embed, text_embed)
    return image_gradient, text_gradient, scale_gradient, bias_gradient, loss


def solution(mesh):
    placed = (P(("blk", "dp"), None), P(("blk", "dp"), None), P(), P())
    return jax.shard_map(
        per_device,
        mesh=mesh,
        in_specs=placed,
        out_specs=(P(("blk", "dp"), None), P(("blk", "dp"), None), P(), P(), P()),
        check_vma=False,
    )
```

time: 718 us -> 145 us (0.20)
  waiting for transfers between devices: 559 us -> 0 us
  Pallas kernels: 0 us -> 133 us
  blocking collectives: 89.8 us -> 0 us
  matrix products: 34.5 us -> 0 us
  between operations: 20.7 us -> 7.18 us
  other arithmetic: 8.68 us -> 0 us
    reduce_scatter x1 -> x0, waiting for transfers between devices: 360 us -> none  [per_device(): lax.psum_scatter(lax.dot_general(coef_all, image_portion, (((0,), (0,)),...]
    all_gather x1 -> x0, waiting for transfers between devices: 199 us -> none  [per_device(): rows_per_block = lax.all_gather(text_half, 'blk', axis=0, tiled=True)]
    pallas_call x0 -> x1, Pallas kernels: none -> 133 us  [per_device(): pl.pallas_call(functools.partial(kernel, pairs), out_shape=(like, like, o...]
    psum x1 -> x0, blocking collectives: 89.8 us -> none  [per_device(): grand_totals = lax.psum((loss_sum, temp_sum, bias_sum), ('blk', 'dp'))]
    dot_general x3 -> x0, matrix products: 34.5 us -> none  [the longest x1 13.6 us: pairwise_losses(): lax.dot_general(local_portion, remote_portion, (((1,), (1,)), ((), ())),...]
  transfers between devices with their start and end apart: 2 -> 0, of which waited for: 2 -> 0; matrix products, arithmetic and copies ran while one was open for 2% -> 0% of each run, Pallas kernels for 0% -> 0%
where the time goes in v1:
time: 145 us; the launch traced here: 144 us
  Pallas kernels  133 us (92%)
  between operations  7.18 us (5%)
  local copies, waits for them, and re-layouts  3.48 us (2%)
    pallas_call x1, Pallas kernels, per_device(): pl.pallas_call(functools.partial(kernel, pairs), out_shape=(like, like, o...  133 us
    unnamed x6, local copies, waits for them, and re-layouts  3.48 us

profile of v1, /device:TPU:33, one launch (start us, length us, event | category | flops | bytes accessed | tf_op | source)
XLA Modules:
  0.0 143.8 jit_solution(541281758058229744)
XLA Ops:
  1.9 0.0 copy-start
  1.9 1.0 copy-done
  2.9 0.0 copy-start.1
  2.9 1.0 copy-done.1
  3.9 133.1 %contrastive_step.1 = (bf16[192,1024]{1,0:T(8,128)(2,1)S(1)}, bf16[192,1024]{1,0:T(8,128)(2,1)S(1)}, f32[1]{0:T(128)}, f32[1]{0:T(128)}, f32[1]{0:T(128)}) custom-call(f32[1]{0:T(128)S(6)} %copy.14.log_scale_ref, f32[1]{0:T(128)S(6)} %copy.15.bias_ref, bf16[192,1024]{1,0:T(8,128)(2,1)S(1)} %copy-done, bf16[192,1024]{1,0:T(8,128)(2,1)S(1)} %copy-done.1), custom_call_target="tpu_custom_call" | custom-call | tf_op jit(solution)/shard_map/contrastive_step/pallas_call | solution.py:319
  137.0 0.7 copy.16
  137.8 0.7 copy.17
Async XLA Ops:
  1.9 1.0 copy-start
  2.9 1.0 copy-start.1

commit v2 on v0

v2 whole, which is shorter than its diff:
```python
import functools

import jax
import jax.numpy as jnp
from jax import lax
from jax.experimental import pallas as pl
from jax.experimental.pallas import tpu as pltpu
from jax.sharding import PartitionSpec as P

EPS = 1e-06
LOG2E = 1.4426950408889634
LN2 = 0.6931471805599453
MESH = pl.DeviceIdType.MESH
SIDE = 4
TILE = 256
TXT, IMG = 0, 1
A, B = 0, 1
OVER_COLS = (((1,), (1,)), ((), ()))
OVER_ROWS = (((0,), (0,)), ((), ()))

Z_IN, GATHER, RELAY, CORE, REDUCE, Z_OUT = 0, 4, 12, 16, 32, 44
ST_X, ST_Y, ST_C, ST_L, ST_P = 48, 51, 54, 55, 58
COPIES = 59


def kernel(
    pairs, log_scale_ref, bias_ref, img_ref, txt_ref,
    out_img, out_txt, out_scale, out_bias, out_loss,
    raw, inverses, texts, images, coef_own, coef_other, cos_even, cos_odd,
    grad_txt, grad_img, recv_txt, recv_img, relay_txt, relay_img,
    final, acc, st_x, st_y, st_c, st_l, st_p, send_sem, recv_sem, local_sem,
):
    rows, width = img_ref.shape
    part = rows // 2
    block = SIDE * part
    share = 2 * block
    blk, dp = lax.axis_index("blk"), lax.axis_index("dp")
    zh, x, y = blk // (SIDE * SIDE), (blk // SIDE) % SIDE, blk % SIDE
    zl, core = dp // 2, dp % 2
    native = core == zh

    def device(dx=0, dy=0, dl=0, other_core=False, other_plane=False):
        h = 1 - zh if other_plane else zh
        c = 1 - core if other_core else core
        return {
            "blk": (h * SIDE + (x + dx) % SIDE) * SIDE + (y + dy) % SIDE,
            "dp": ((zl + dl) % SIDE) * 2 + c,
        }

    along_x = [device(dx=d) for d in (1, 2, 3)]
    along_y = [device(dy=d) for d in (1, 2, 3)]
    along_l = [device(dl=d) for d in (1, 2, 3)]
    right = (along_x[0], along_y[0])
    left = (along_x[2], along_y[2])
    sibling = device(other_core=True)
    partner = device(other_core=True, other_plane=True)
    inputs, outputs = (txt_ref, img_ref), (out_txt, out_img)
    units, grads = (texts, images), (grad_txt, grad_img)
    recvs, relays = (recv_txt, recv_img), (relay_txt, relay_img)

    def copy(number, src, dst, where):
        return pltpu.make_async_remote_copy(
            src_ref=src, dst_ref=dst, send_sem=send_sem.at[number], recv_sem=recv_sem.at[number],
            device_id=where, device_id_type=MESH,
        )

    def half(h):
        return pl.ds(h * part, part)

    def slot(h, index, other=0):
        return pl.ds(other * share + h * block + index * part, part)

    def z_in(t, h):
        return copy(Z_IN + 2 * t + h, inputs[t].at[half(h)], raw.at[t, half(h)], partner)

    def gather(t, h, d):
        return copy(
            GATHER + 4 * t + 2 * h + d, units[t].at[slot(h, 0)], units[t].at[slot(h, (3, 1)[d])], (right, left)[d][t]
        )

    def relay(t, h):
        return copy(
            RELAY + 2 * t + h, units[t].at[slot(h, (3, 1)[h])], units[t].at[slot(h, 2)], (right, left)[h][t]
        )

    def to_core(t, h, index):
        return copy(
            CORE + 8 * t + 4 * h + index, units[t].at[slot(h, index)], units[t].at[slot(h, index, 1)], sibling
        )

    def reduce(t, h, step):
        onward = step != 1
        to = (right, left)[h if onward else 1 - h][t]
        if step == 0:
            src, dst = slot(h, 2), relays[t].at[h]
        elif step == 1:
            src, dst = slot(h, (3, 1)[h]), recvs[t].at[1 - h, half(h)]
        else:
            src, dst = slot(h, (1, 3)[h]), recvs[t].at[h, half(h)]
        return copy(REDUCE + 6 * t + 3 * h + step, grads[t].at[src], dst, to)

    def z_out(t, h):
        return copy(Z_OUT + 2 * t + h, final.at[t, half(h)], outputs[t].at[half(h)], partner)

    def local_in(t):
        return pltpu.make_async_copy(inputs[t], raw.at[t], local_sem.at[t])

    def local_out(t, h):
        return pltpu.make_async_copy(final.at[t, half(h)], outputs[t].at[half(h)], local_sem.at[2 + 2 * t + h])

    @pl.when(native)
    def _():
        local_in(TXT).start()
        local_in(IMG).start()

    barrier = pltpu.get_barrier_semaphore()
    everyone = along_x + along_y + along_l + [sibling, partner]
    for other in everyone:
        pl.semaphore_signal(barrier, inc=1, device_id=other, device_id_type=MESH)
    pl.semaphore_wait(barrier, len(everyone))

    log_scale = jnp.full((1, TILE), log_scale_ref[0], jnp.float32)
    scale = jnp.exp(log_scale)
    scale2 = scale * LOG2E
    bias2 = jnp.full((1, TILE), bias_ref[0], jnp.float32) * LOG2E
    acc[...] = jnp.zeros_like(acc)

    def normalize(t, h):
        for i in range(part // 32):
            at = pl.ds(h * part + i * 32, 32)
            wide = raw[t, at, :].astype(jnp.float32)
            inverse = lax.rsqrt(jnp.sum(wide * wide, axis=1, keepdims=True) + EPS)
            inverses[t, at, :] = jnp.broadcast_to(inverse, (32, 128))
            units[t][pl.ds(h * block + i * 32, 32), :] = (wide * inverse).astype(jnp.bfloat16)

    def send_half(t, h):
        normalize(t, h)
        gather(t, h, h).start()
        gather(t, h, 1 - h).start()
        to_core(t, h, 0).start()

    def pass_on(t, h):
        gather(t, h, h).wait_recv()
        relay(t, h).start()
        to_core(t, h, (3, 1)[h]).start()
        gather(t, h, 1 - h).wait_recv()
        to_core(t, h, (1, 3)[h]).start()

    def pass_last(t, h):
        relay(t, h).wait_recv()
        to_core(t, h, 2).start()

    def from_core(t, h):
        for index in range(SIDE):
            to_core(t, h, index).wait_recv()

    def dot_tile(out, first, column):
        out[...] = lax.dot_general(
            images[pl.ds(first, block), :],
            texts[pl.ds(pl.multiple_of(column * TILE, TILE), TILE), :],
            OVER_COLS,
            preferred_element_type=jnp.float32,
        )

    def own_terms(cos_ref, h, column):
        at_cols = pl.ds(pl.multiple_of(column * TILE, TILE), TILE)
        losses = temps = biases = jnp.zeros((8, TILE), jnp.float32)
        strip = 16
        for i in range(block // strip):
            cosine = cos_ref[pl.ds(i * strip, strip), :]
            grown = jnp.exp2(scale2 * cosine + bias2)
            more = 1.0 + grown
            coef = grown / more
            coef_own[pl.ds(h * block + i * strip, strip), at_cols] = coef.astype(jnp.bfloat16)
            fold = (strip // 8, 8, TILE)
            losses += jnp.sum(jnp.log(more).reshape(fold), axis=0)
            temps += jnp.sum((coef * cosine).reshape(fold), axis=0)
            biases += jnp.sum(coef.reshape(fold), axis=0)
        acc[0] += losses
        acc[1] += temps
        acc[2] += biases

    def other_terms(cos_ref, h, column):
        at_cols = pl.ds(pl.multiple_of(column * TILE, TILE), TILE)
        strip = 16
        for i in range(block // strip):
            grown = jnp.exp2(scale2 * cos_ref[pl.ds(i * strip, strip), :] + bias2)
            coef_other[pl.ds(h * block + i * strip, strip), at_cols] = (grown / (1.0 + grown)).astype(jnp.bfloat16)

    def sweep(terms, first, h, start, stop):
        dot_tile(cos_even, first, start)
        count = stop - start

        def body(p, _):
            column = start + 2 * p
            dot_tile(cos_odd, first, column + 1)
            terms(cos_even, h, column)
            dot_tile(cos_even, first, jnp.minimum(column + 2, stop - 1))
            terms(cos_odd, h, column + 1)
            return 0

        lax.fori_loop(0, count // 2, body, 0)
        if count % 2:
            terms(cos_even, h, stop - 1)

    def own_logits(h, start, stop):
        sweep(own_terms, h * block, h, start, stop)

    def other_logits(h):
        sweep(other_terms, share + h * block, h, 0, share // TILE)

    def same_pairs(h):
        lanes = 128
        at_rows, at_cols = pl.ds(h * block, part), pl.ds(h * block, lanes)
        cosine = lax.dot_general(
            images[at_rows, :], texts[at_cols, :], OVER_COLS, preferred_element_type=jnp.float32
        )
        shape = (part, lanes)
        same = lax.broadcasted_iota(jnp.int32, shape, 0) == lax.broadcasted_iota(jnp.int32, shape, 1)
        grown = jnp.exp2(scale2[:, :lanes] * cosine + bias2[:, :lanes])
        more = 1.0 + grown
        inverse = 1.0 / more
        coef = grown * inverse
        coef_own[at_rows, at_cols] = jnp.where(same, -inverse, coef).astype(jnp.bfloat16)
        logit = scale[:, :lanes] * cosine + bias_ref[0]
        change = jnp.where(same, -inverse - coef, 0.0)
        fold = (part // 8, 8, lanes)
        acc[0, :, :lanes] += jnp.sum(jnp.where(same, -logit, 0.0).reshape(fold), axis=0)
        acc[1, :, :lanes] += jnp.sum((change * cosine).reshape(fold), axis=0)
        acc[2, :, :lanes] += jnp.sum(change.reshape(fold), axis=0)

    def image_terms(h):
        def column(n, _):
            at = pl.ds(pl.multiple_of(n * TILE, TILE), TILE)
            grad_img[pl.ds(h * block, block), at] = jnp.dot(
                coef_own[pl.ds(h * block, block), :], texts[:, at], preferred_element_type=jnp.float32
            )
            return 0

        lax.fori_loop(0, width // TILE, column, 0)
        reduce(IMG, h, 0).start()
        reduce(IMG, h, 1).start()

    def text_terms(h):
        at_rows = pl.ds(h * block, block)

        def column(n, _):
            at = pl.ds(pl.multiple_of(n * TILE, TILE), TILE)
            grad_txt[at_rows, at] = lax.dot_general(
                coef_own[:, at_rows], images[:share, at], OVER_ROWS, preferred_element_type=jnp.float32
            ) + lax.dot_general(
                coef_other[:, at_rows], images[share:, at], OVER_ROWS, preferred_element_type=jnp.float32
            )
            return 0

        lax.fori_loop(0, width // TILE, column, 0)
        reduce(TXT, h, 0).start()
        reduce(TXT, h, 1).start()

    def add_relayed(t, h):
        reduce(t, h, 0).wait_recv()
        grads[t][slot(h, (1, 3)[h]), :] += relays[t][h]
        reduce(t, h, 2).start()

    def finish(t, h):
        reduce(t, h, 1).wait_recv()
        reduce(t, h, 2).wait_recv()
        for i in range(part // 16):
            at = pl.ds(h * part + i * 16, 16)
            inverse = inverses[t, at, :1]
            unit = raw[t, at, :].astype(jnp.float32) * inverse
            scaled = scale[:, :1] * (
                grads[t][pl.ds(h * block + i * 16, 16), :] + recvs[t][0, at, :] + recvs[t][1, at, :]
            )
            along = jnp.sum(unit * scaled, axis=1, keepdims=True)
            final[t, at, :] = ((scaled - unit * along) * inverse).astype(jnp.bfloat16)

    stages = (
        (ST_X, st_x, x, along_x),
        (ST_Y, st_y, y, along_y),
        (ST_C, st_c, core, [sibling]),
        (ST_L, st_l, zl, along_l),
        (ST_P, st_p, zh, [partner]),
    )

    def stage_copies(base, buffer, mine, line):
        return [copy(base + i, buffer.at[mine], buffer.at[mine], other) for i, other in enumerate(line)]

    def sums_start(stage, value):
        _, buffer, mine, _ = stages[stage]
        buffer[mine] = value
        for each in stage_copies(*stages[stage]):
            each.start()

    def sums_finish(stage):
        for each in stage_copies(*stages[stage]):
            each.wait_recv()
        buffer, count = stages[stage][1], len(stages[stage][3]) + 1
        return functools.reduce(lambda a, b: a + b, [buffer[i] for i in range(count)])

    def sums_first():
        sums_start(0, (acc[:, :, :128] + acc[:, :, 128:]).reshape(24, 128))

    def sums_next(stage):
        sums_start(stage, sums_finish(stage - 1))

    def sums_last():
        totals = sums_finish(len(stages) - 1)
        loss_sum, temp_sum, bias_sum = (
            jnp.sum(jnp.sum(totals[8 * k : 8 * k + 8], axis=0, keepdims=True), axis=1, keepdims=True)
            for k in range(3)
        )
        out_loss[0] = (loss_sum / pairs)[0, 0]
        out_scale[0] = (scale[:, :1] * temp_sum / pairs)[0, 0]
        out_bias[0] = (bias_sum / pairs)[0, 0]

    tiles = share // TILE

    @pl.when(native)
    def _():
        for t in (TXT, IMG):
            local_in(t).wait()
            send_half(t, A)
            send_half(t, B)
        for t in (TXT, IMG):
            pass_on(t, A)
            pass_on(t, B)
            pass_last(t, A)
            pass_last(t, B)
        own_logits(A, 0, tiles)
        own_logits(B, 0, tiles)
        from_core(TXT, A)
        from_core(TXT, B)
        own_logits(A, tiles, 2 * tiles)
        same_pairs(A)
        image_terms(A)
        own_logits(B, tiles, 2 * tiles)
        same_pairs(B)
        image_terms(B)
        sums_first()
        add_relayed(IMG, A)
        add_relayed(IMG, B)
        from_core(IMG, A)
        other_logits(A)
        from_core(IMG, B)
        other_logits(B)
        text_terms(A)
        sums_next(1)
        text_terms(B)
        sums_next(2)
        add_relayed(TXT, A)
        sums_next(3)
        add_relayed(TXT, B)
        sums_next(4)
        for t in (IMG, TXT):
            for h in (A, B):
                finish(t, h)
                local_out(t, h).start()
        sums_last()
        for t in (IMG, TXT):
            for h in (A, B):
                local_out(t, h).wait()

    @pl.when(jnp.logical_not(native))
    def _():
        z_in(TXT, A).start()
        z_in(TXT, A).wait_send()
        z_in(TXT, B).start()
        z_in(TXT, A).wait_recv()
        send_half(TXT, A)
        z_in(TXT, B).wait_send()
        z_in(IMG, A).start()
        pass_on(TXT, A)
        z_in(TXT, B).wait_recv()
        send_half(TXT, B)
        z_in(IMG, A).wait_send()
        z_in(IMG, B).start()
        pass_last(TXT, A)
        pass_on(TXT, B)
        pass_last(TXT, B)
        from_core(IMG, A)
        from_core(IMG, B)
        other_logits(A)
        z_in(IMG, A).wait_recv()
        send_half(IMG, A)
        other_logits(B)
        from_core(TXT, A)
        from_core(TXT, B)
        pass_on(IMG, A)
        z_in(IMG, B).wait_recv()
        send_half(IMG, B)
        pass_last(IMG, A)
        own_logits(A, 0, tiles)
        pass_on(IMG, B)
        own_logits(A, tiles, 2 * tiles)
        pass_last(IMG, B)
        same_pairs(A)
        image_terms(A)
        own_logits(B, 0, 2 * tiles)
        same_pairs(B)
        text_terms(A)
        sums_first()
        text_terms(B)
        add_relayed(IMG, A)
        image_terms(B)
        sums_next(1)
        add_relayed(TXT, A)
        add_relayed(TXT, B)
        sums_next(2)
        add_relayed(IMG, B)
        sums_next(3)
        finish(IMG, A)
        z_out(IMG, A).start()
        finish(TXT, A)
        z_out(TXT, A).start()
        sums_next(4)
        finish(TXT, B)
        z_out(TXT, B).start()
        finish(IMG, B)
        z_out(IMG, B).start()
        sums_last()
        z_in(IMG, B).wait_send()
        for t in (IMG, TXT):
            for h in (A, B):
                z_out(t, h).wait()

    for t in (TXT, IMG):
        for h in (A, B):
            gather(t, h, 0).wait_send()
            gather(t, h, 1).wait_send()
            relay(t, h).wait_send()
            for index in range(SIDE):
                to_core(t, h, index).wait_send()
            for step in range(3):
                reduce(t, h, step).wait_send()
    for stage in stages:
        for each in stage_copies(*stage):
            each.wait_send()


def per_device(image_embed, text_embed, log_logit_scale, logit_bias):
    rows, width = image_embed.shape
    share = SIDE * rows
    block = share // 2
    pairs = rows * lax.axis_size("blk") * lax.axis_size("dp")
    anywhere, smem = pl.BlockSpec(memory_space=pl.ANY), pl.BlockSpec(memory_space=pltpu.SMEM)
    one = jax.ShapeDtypeStruct((1,), jnp.float32)
    like = jax.ShapeDtypeStruct((rows, width), jnp.bfloat16)
    bf16, f32 = jnp.bfloat16, jnp.float32
    image_gradient, text_gradient, scale_gradient, bias_gradient, loss = pl.pallas_call(
        functools.partial(kernel, pairs),
        out_shape=(like, like, one, one, one),
        in_specs=[smem, smem, anywhere, anywhere],
        out_specs=(anywhere, anywhere, smem, smem, smem),
        scratch_shapes=[
            pltpu.VMEM((2, rows, width), bf16),
            pltpu.VMEM((2, rows, 128), f32),
            pltpu.VMEM((2 * share, width), bf16),
            pltpu.VMEM((2 * share, width), bf16),
            pltpu.VMEM((share, 2 * share), bf16),
            pltpu.VMEM((share, share), bf16),
            pltpu.VMEM((block, TILE), f32),
            pltpu.VMEM((block, TILE), f32),
            pltpu.VMEM((share, width), f32),
            pltpu.VMEM((share, width), f32),
            pltpu.VMEM((2, rows, width), f32),
            pltpu.VMEM((2, rows, width), f32),
            pltpu.VMEM((2, rows // 2, width), f32),
            pltpu.VMEM((2, rows // 2, width), f32),
            pltpu.VMEM((2, rows, width), bf16),
            pltpu.VMEM((3, 8, TILE), f32),
            pltpu.VMEM((4, 24, 128), f32),
            pltpu.VMEM((4, 24, 128), f32),
            pltpu.VMEM((2, 24, 128), f32),
            pltpu.VMEM((4, 24, 128), f32),
            pltpu.VMEM((2, 24, 128), f32),
            pltpu.SemaphoreType.DMA((COPIES,)),
            pltpu.SemaphoreType.DMA((COPIES,)),
            pltpu.SemaphoreType.DMA((6,)),
        ],
        name="contrastive_step",
        compiler_params=pltpu.CompilerParams(
            collective_id=0, has_side_effects=True, vmem_limit_bytes=48 * 2**20
        ),
    )(log_logit_scale, logit_bias, image_embed, text_embed)
    return image_gradient, text_gradient, scale_gradient, bias_gradient, loss


def solution(mesh):
    placed = (P(("blk", "dp"), None), P(("blk", "dp"), None), P(), P())
    return jax.shard_map(
        per_device,
        mesh=mesh,
        in_specs=placed,
        out_specs=(P(("blk", "dp"), None), P(("blk", "dp"), None), P(), P(), P()),
        check_vma=False,
    )
```

time: 718 us -> 115 us (0.16)
  waiting for transfers between devices: 559 us -> 0 us
  Pallas kernels: 0 us -> 103 us
  blocking collectives: 89.8 us -> 0 us
  matrix products: 34.5 us -> 0 us
  between operations: 20.7 us -> 7.18 us
  other arithmetic: 8.68 us -> 0 us
    reduce_scatter x1 -> x0, waiting for transfers between devices: 360 us -> none  [per_device(): lax.psum_scatter(lax.dot_general(coef_all, image_portion, (((0,), (0,)),...]
    all_gather x1 -> x0, waiting for transfers between devices: 199 us -> none  [per_device(): rows_per_block = lax.all_gather(text_half, 'blk', axis=0, tiled=True)]
    pallas_call x0 -> x1, Pallas kernels: none -> 103 us  [per_device(): pl.pallas_call(functools.partial(kernel, pairs), out_shape=(like, like, o...]
    psum x1 -> x0, blocking collectives: 89.8 us -> none  [per_device(): grand_totals = lax.psum((loss_sum, temp_sum, bias_sum), ('blk', 'dp'))]
    dot_general x3 -> x0, matrix products: 34.5 us -> none  [the longest x1 13.6 us: pairwise_losses(): lax.dot_general(local_portion, remote_portion, (((1,), (1,)), ((), ())),...]
  transfers between devices with their start and end apart: 2 -> 0, of which waited for: 2 -> 0; matrix products, arithmetic and copies ran while one was open for 2% -> 0% of each run, Pallas kernels for 0% -> 0%
where the time goes in v2:
time: 115 us; the launch traced here: 113 us
  Pallas kernels  103 us (90%)
  between operations  7.18 us (6%)
  local copies, waits for them, and re-layouts  3.48 us (3%)
    pallas_call x1, Pallas kernels, per_device(): pl.pallas_call(functools.partial(kernel, pairs), out_shape=(like, like, o...  103 us
    unnamed x6, local copies, waits for them, and re-layouts  3.48 us

profile of v2, /device:TPU:33, one launch (start us, length us, event | category | flops | bytes accessed | tf_op | source)
XLA Modules:
  0.0 113.4 jit_solution(168631572210614838)
XLA Ops:
  1.9 0.0 copy-start
  1.9 1.0 copy-done
  2.9 0.0 copy-start.1
  2.9 1.0 copy-done.1
  3.9 102.7 %contrastive_step.1 = (bf16[192,1024]{1,0:T(8,128)(2,1)S(1)}, bf16[192,1024]{1,0:T(8,128)(2,1)S(1)}, f32[1]{0:T(128)}, f32[1]{0:T(128)}, f32[1]{0:T(128)}) custom-call(f32[1]{0:T(128)S(6)} %copy.14.log_scale_ref, f32[1]{0:T(128)S(6)} %copy.15.bias_ref, bf16[192,1024]{1,0:T(8,128)(2,1)S(1)} %copy-done, bf16[192,1024]{1,0:T(8,128)(2,1)S(1)} %copy-done.1), custom_call_target="tpu_custom_call" | custom-call | tf_op jit(solution)/shard_map/contrastive_step/pallas_call | solution.py:450
  106.7 0.7 copy.16
  107.4 0.7 copy.17
Async XLA Ops:
  1.9 1.0 copy-start
  2.9 1.0 copy-start.1

commit v3 on v2

--- a/solution.py
+++ b/solution.py
@@ -24,11 +24,11 @@
 
 
 def kernel(
-    pairs, log_scale_ref, bias_ref, img_ref, txt_ref,
-    out_img, out_txt, out_scale, out_bias, out_loss,
+    pairs, log_scale_any, bias_any, img_ref, txt_ref,
+    out_img, out_txt, out_totals,
     raw, inverses, texts, images, coef_own, coef_other, cos_even, cos_odd,
     grad_txt, grad_img, recv_txt, recv_img, relay_txt, relay_img,
-    final, acc, st_x, st_y, st_c, st_l, st_p, send_sem, recv_sem, local_sem,
+    final, acc, st_x, st_y, st_c, st_l, st_p, log_scale_ref, bias_ref, send_sem, recv_sem, local_sem, turn,
 ):
     rows, width = img_ref.shape
     part = rows // 2
@@ -108,6 +108,13 @@
     def local_out(t, h):
         return pltpu.make_async_copy(final.at[t, half(h)], outputs[t].at[half(h)], local_sem.at[2 + 2 * t + h])
 
+    scalar_copies = [
+        pltpu.make_async_copy(src, dst, local_sem.at[6 + i])
+        for i, (src, dst) in enumerate(((log_scale_any, log_scale_ref), (bias_any, bias_ref)))
+    ]
+    for each in scalar_copies:
+        each.start()
+
     @pl.when(native)
     def _():
         local_in(TXT).start()
@@ -119,6 +126,8 @@
         pl.semaphore_signal(barrier, inc=1, device_id=other, device_id_type=MESH)
     pl.semaphore_wait(barrier, len(everyone))
 
+    for each in scalar_copies:
+        each.wait()
     log_scale = jnp.full((1, TILE), log_scale_ref[0], jnp.float32)
     scale = jnp.exp(log_scale)
     scale2 = scale * LOG2E
@@ -230,30 +239,20 @@
         acc[2, :, :lanes] += jnp.sum(change.reshape(fold), axis=0)
 
     def image_terms(h):
-        def column(n, _):
-            at = pl.ds(pl.multiple_of(n * TILE, TILE), TILE)
-            grad_img[pl.ds(h * block, block), at] = jnp.dot(
-                coef_own[pl.ds(h * block, block), :], texts[:, at], preferred_element_type=jnp.float32
-            )
-            return 0
-
-        lax.fori_loop(0, width // TILE, column, 0)
+        at_rows = pl.ds(h * block, block)
+        grad_img[at_rows, :] = jnp.dot(coef_own[at_rows, :], texts[...], preferred_element_type=jnp.float32)
         reduce(IMG, h, 0).start()
         reduce(IMG, h, 1).start()
 
     def text_terms(h):
         at_rows = pl.ds(h * block, block)
-
-        def column(n, _):
-            at = pl.ds(pl.multiple_of(n * TILE, TILE), TILE)
-            grad_txt[at_rows, at] = lax.dot_general(
-                coef_own[:, at_rows], images[:share, at], OVER_ROWS, preferred_element_type=jnp.float32
-            ) + lax.dot_general(
-                coef_other[:, at_rows], images[share:, at], OVER_ROWS, preferred_element_type=jnp.float32
-            )
-            return 0
-
-        lax.fori_loop(0, width // TILE, column, 0)
+        grad_txt[at_rows, :] = lax.dot_general(
+            coef_own[:, at_rows], images[:share, :], OVER_ROWS, preferred_element_type=jnp.float32
+        ) + lax.dot_general(
+            coef_other[:, at_rows], images[share:, :], OVER_ROWS, preferred_element_type=jnp.float32
+        )
+
+    def text_start(h):
         reduce(TXT, h, 0).start()
         reduce(TXT, h, 1).start()
 
@@ -306,15 +305,16 @@
 
     def sums_last():
         totals = sums_finish(len(stages) - 1)
-        loss_sum, temp_sum, bias_sum = (
-            jnp.sum(jnp.sum(totals[8 * k : 8 * k + 8], axis=0, keepdims=True), axis=1, keepdims=True)
-            for k in range(3)
-        )
-        out_loss[0] = (loss_sum / pairs)[0, 0]
-        out_scale[0] = (scale[:, :1] * temp_sum / pairs)[0, 0]
-        out_bias[0] = (bias_sum / pairs)[0, 0]
+        for k, factor in enumerate((1.0, scale[:, :1], 1.0)):
+            total = jnp.sum(jnp.sum(totals[8 * k : 8 * k + 8], axis=0, keepdims=True), axis=1, keepdims=True)
+            out_totals[k : k + 1, :] = jnp.broadcast_to(factor * total / pairs, (1, 128))
 
     tiles = share // TILE
+
+    def wait_sent(t, steps):
+        for h in (A, B):
+            for step in steps:
+                reduce(t, h, step).wait_send()
 
     @pl.when(native)
     def _():
@@ -342,24 +342,30 @@
         add_relayed(IMG, B)
         from_core(IMG, A)
         other_logits(A)
+        sums_next(1)
         from_core(IMG, B)
         other_logits(B)
         text_terms(A)
-        sums_next(1)
         text_terms(B)
         sums_next(2)
+        for h in (A, B):
+            finish(IMG, h)
+            local_out(IMG, h).start()
+        pl.semaphore_wait(turn, 1)
+        text_start(A)
+        text_start(B)
+        sums_next(3)
         add_relayed(TXT, A)
-        sums_next(3)
         add_relayed(TXT, B)
         sums_next(4)
-        for t in (IMG, TXT):
-            for h in (A, B):
-                finish(t, h)
-                local_out(t, h).start()
+        for h in (A, B):
+            finish(TXT, h)
+            local_out(TXT, h).start()
         sums_last()
         for t in (IMG, TXT):
             for h in (A, B):
                 local_out(t, h).wait()
+        wait_sent(TXT, (2,))
 
     @pl.when(jnp.logical_not(native))
     def _():
@@ -376,48 +382,52 @@
         z_in(IMG, A).wait_send()
         z_in(IMG, B).start()
         pass_last(TXT, A)
+        z_in(IMG, A).wait_recv()
+        send_half(IMG, A)
         pass_on(TXT, B)
+        z_in(IMG, B).wait_recv()
+        send_half(IMG, B)
+        pass_on(IMG, A)
         pass_last(TXT, B)
         from_core(IMG, A)
         from_core(IMG, B)
         other_logits(A)
-        z_in(IMG, A).wait_recv()
-        send_half(IMG, A)
         other_logits(B)
         from_core(TXT, A)
         from_core(TXT, B)
-        pass_on(IMG, A)
-        z_in(IMG, B).wait_recv()
-        send_half(IMG, B)
         pass_last(IMG, A)
         own_logits(A, 0, tiles)
         pass_on(IMG, B)
         own_logits(A, tiles, 2 * tiles)
+        same_pairs(A)
         pass_last(IMG, B)
-        same_pairs(A)
         image_terms(A)
         own_logits(B, 0, 2 * tiles)
         same_pairs(B)
         text_terms(A)
+        text_start(A)
+        text_terms(B)
+        text_start(B)
         sums_first()
-        text_terms(B)
         add_relayed(IMG, A)
         image_terms(B)
-        sums_next(1)
         add_relayed(TXT, A)
         add_relayed(TXT, B)
-        sums_next(2)
+        sums_next(1)
         add_relayed(IMG, B)
-        sums_next(3)
         finish(IMG, A)
         z_out(IMG, A).start()
+        sums_next(2)
+        wait_sent(TXT, (2,))
+        pl.semaphore_signal(turn, inc=1, device_id=sibling, device_id_type=MESH)
         finish(TXT, A)
         z_out(TXT, A).start()
-        sums_next(4)
         finish(TXT, B)
         z_out(TXT, B).start()
         finish(IMG, B)
         z_out(IMG, B).start()
+        sums_next(3)
+        sums_next(4)
         sums_last()
         z_in(IMG, B).wait_send()
         for t in (IMG, TXT):
@@ -431,8 +441,8 @@
             relay(t, h).wait_send()
             for index in range(SIDE):
                 to_core(t, h, index).wait_send()
-            for step in range(3):
-                reduce(t, h, step).wait_send()
+    wait_sent(TXT, (0, 1))
+    wait_sent(IMG, (0, 1, 2))
     for stage in stages:
         for each in stage_copies(*stage):
             each.wait_send()
@@ -443,15 +453,14 @@
     share = SIDE * rows
     block = share // 2
     pairs = rows * lax.axis_size("blk") * lax.axis_size("dp")
-    anywhere, smem = pl.BlockSpec(memory_space=pl.ANY), pl.BlockSpec(memory_space=pltpu.SMEM)
-    one = jax.ShapeDtypeStruct((1,), jnp.float32)
+    hbm, vmem = pl.BlockSpec(memory_space=pltpu.HBM), pl.BlockSpec(memory_space=pltpu.VMEM)
     like = jax.ShapeDtypeStruct((rows, width), jnp.bfloat16)
     bf16, f32 = jnp.bfloat16, jnp.float32
-    image_gradient, text_gradient, scale_gradient, bias_gradient, loss = pl.pallas_call(
+    image_gradient, text_gradient, totals = pl.pallas_call(
         functools.partial(kernel, pairs),
-        out_shape=(like, like, one, one, one),
-        in_specs=[smem, smem, anywhere, anywhere],
-        out_specs=(anywhere, anywhere, smem, smem, smem),
+        out_shape=(like, like, jax.ShapeDtypeStruct((8, 128), f32)),
+        in_specs=[hbm, hbm, hbm, hbm],
+        out_specs=(hbm, hbm, vmem),
         scratch_shapes=[
             pltpu.VMEM((2, rows, width), bf16),
             pltpu.VMEM((2, rows, 128), f32),
@@ -474,15 +483,19 @@
             pltpu.VMEM((2, 24, 128), f32),
             pltpu.VMEM((4, 24, 128), f32),
             pltpu.VMEM((2, 24, 128), f32),
+            pltpu.SMEM((1,), f32),
+            pltpu.SMEM((1,), f32),
             pltpu.SemaphoreType.DMA((COPIES,)),
             pltpu.SemaphoreType.DMA((COPIES,)),
-            pltpu.SemaphoreType.DMA((6,)),
+            pltpu.SemaphoreType.DMA((8,)),
+            pltpu.SemaphoreType.REGULAR,
         ],
         name="contrastive_step",
         compiler_params=pltpu.CompilerParams(
-            collective_id=0, has_side_effects=True, vmem_limit_bytes=48 * 2**20
+            collective_id=0, has_side_effects=True, vmem_limit_bytes=62 * 2**20
         ),
     )(log_logit_scale, logit_bias, image_embed, text_embed)
+    loss, scale_gradient, bias_gradient = totals[0, :1], totals[1, :1], totals[2, :1]
     return image_gradient, text_gradient, scale_gradient, bias_gradient, loss
 
 

time: 115 us -> 100 us (0.87)
  the two profiles are of different devices: /device:TPU:33 before, /device:TPU:1 now
where the time goes in v3:
time: 100 us
  Pallas kernels  94.2 us (94%)
  local copies, waits for them, and re-layouts  3.87 us (4%)
  between operations  1.93 us (2%)
    pallas_call x1, Pallas kernels, per_device(): pl.pallas_call(functools.partial(kernel, pairs), out_shape=(like, like, j...  94.2 us
    unnamed x4, local copies, waits for them, and re-layouts  2.57 us

profile of v3, /device:TPU:1, one launch (start us, length us, event | category | flops | bytes accessed | tf_op | source)
XLA Modules:
  0.0 100.0 jit_solution(13111430681210171184)
XLA Ops:
  1.9 94.2 %contrastive_step.1 = (bf16[192,1024]{1,0:T(8,128)(2,1)}, bf16[192,1024]{1,0:T(8,128)(2,1)}, f32[8,128]{1,0:T(8,128)}) custom-call(f32[1]{0:T(128)S(6)} %copy.11.log_scale_any, f32[1]{0:T(128)S(6)} %copy.12.bias_any, bf16[192,1024]{1,0:T(8,128)(2,1)} %img_ref.1, bf16[192,1024]{1,0:T(8,128)(2,1)} %txt_ref.1), custom_call_target="tpu_custom_call" | custom-call | tf_op jit(solution)/shard_map/contrastive_step/pallas_call | solution.py:459
  96.2 1.3 %fusion = (f32[1,1]{1,0:T(1,128)}, f32[1,1]{1,0:T(1,128)}, f32[1,1]{1,0:T(1,128)}) fusion(f32[8,128]{1,0:T(8,128)} %get-tuple-element.10), kind=kLoop, calls=%fused_computation | loop fusion | bytes 24 | tf_op jit(solution)/shard_map/slice | solution.py:498
  97.5 0.0 copy-start
  97.5 1.8 %copy.13 = bf16[192,1024]{1,0:T(8,128)(2,1)} copy(bf16[192,1024]{1,0:T(8,128)(2,1)} %get-tuple-element.19) | data formatting | bytes 786432
  99.3 0.0 copy-done
  99.3 0.7 copy.14
Async XLA Ops:
  97.5 1.8 %copy-start = (bf16[192,1024]{1,0:T(8,128)(2,1)S(1)}, bf16[192,1024]{1,0:T(8,128)(2,1)}, u32[]{:S(2)}) copy-start(bf16[192,1024]{1,0:T(8,128)(2,1)} %get-tuple-element.20) | copy-start | bytes 1179652

commit v4 on v3

--- a/solution.py
+++ b/solution.py
@@ -18,9 +18,9 @@
 OVER_COLS = (((1,), (1,)), ((), ()))
 OVER_ROWS = (((0,), (0,)), ((), ()))
 
-Z_IN, GATHER, RELAY, CORE, REDUCE, Z_OUT = 0, 4, 12, 16, 32, 44
-ST_X, ST_Y, ST_C, ST_L, ST_P = 48, 51, 54, 55, 58
-COPIES = 59
+Z_IN, GATHER, ACROSS, CORE, REDUCE, Z_OUT = 0, 4, 12, 16, 32, 44
+ST_X, ST_Y, ST_C, ST_L, ST_P = 48, 51, 54, 56, 59
+COPIES = 60
 
 
 def kernel(
@@ -78,9 +78,9 @@
             GATHER + 4 * t + 2 * h + d, units[t].at[slot(h, 0)], units[t].at[slot(h, (3, 1)[d])], (right, left)[d][t]
         )
 
-    def relay(t, h):
+    def across(t, h):
         return copy(
-            RELAY + 2 * t + h, units[t].at[slot(h, (3, 1)[h])], units[t].at[slot(h, 2)], (right, left)[h][t]
+            ACROSS + 2 * t + h, units[t].at[slot(h, 0)], units[t].at[slot(h, 2)], (along_x, along_y)[t][1]
         )
 
     def to_core(t, h, index):
@@ -144,20 +144,15 @@
 
     def send_half(t, h):
         normalize(t, h)
-        gather(t, h, h).start()
-        gather(t, h, 1 - h).start()
+        across(t, h).start()
+        gather(t, h, 0).start()
+        gather(t, h, 1).start()
         to_core(t, h, 0).start()
 
     def pass_on(t, h):
-        gather(t, h, h).wait_recv()
-        relay(t, h).start()
-        to_core(t, h, (3, 1)[h]).start()
-        gather(t, h, 1 - h).wait_recv()
-        to_core(t, h, (1, 3)[h]).start()
-
-    def pass_last(t, h):
-        relay(t, h).wait_recv()
-        to_core(t, h, 2).start()
+        for index, landed in ((3, gather(t, h, 0)), (1, gather(t, h, 1)), (2, across(t, h))):
+            landed.wait_recv()
+            to_core(t, h, index).start()
 
     def from_core(t, h):
         for index in range(SIDE):
@@ -241,20 +236,25 @@
     def image_terms(h):
         at_rows = pl.ds(h * block, block)
         grad_img[at_rows, :] = jnp.dot(coef_own[at_rows, :], texts[...], preferred_element_type=jnp.float32)
-        reduce(IMG, h, 0).start()
-        reduce(IMG, h, 1).start()
+
+    def turned_dot(coefs, units_rows):
+        return lax.dot_general(coefs, units_rows, OVER_ROWS, preferred_element_type=jnp.float32)
+
+    def text_early(h):
+        at_rows = pl.ds(h * block, block)
+        grad_txt[at_rows, :] = turned_dot(coef_own[:block, at_rows], images[:block, :]) + turned_dot(
+            coef_other[:, at_rows], images[share:, :]
+        )
+
+    def text_late(h):
+        at_rows = pl.ds(h * block, block)
+        grad_txt[at_rows, :] += turned_dot(coef_own[block:, at_rows], images[block:share, :])
 
     def text_terms(h):
         at_rows = pl.ds(h * block, block)
-        grad_txt[at_rows, :] = lax.dot_general(
-            coef_own[:, at_rows], images[:share, :], OVER_ROWS, preferred_element_type=jnp.float32
-        ) + lax.dot_general(
-            coef_other[:, at_rows], images[share:, :], OVER_ROWS, preferred_element_type=jnp.float32
-        )
-
-    def text_start(h):
-        reduce(TXT, h, 0).start()
-        reduce(TXT, h, 1).start()
+        grad_txt[at_rows, :] = turned_dot(coef_own[:, at_rows], images[:share, :]) + turned_dot(
+            coef_other[:, at_rows], images[share:, :]
+        )
 
     def add_relayed(t, h):
         reduce(t, h, 0).wait_recv()
@@ -274,13 +274,12 @@
             along = jnp.sum(unit * scaled, axis=1, keepdims=True)
             final[t, at, :] = ((scaled - unit * along) * inverse).astype(jnp.bfloat16)
 
-    stages = (
-        (ST_X, st_x, x, along_x),
-        (ST_Y, st_y, y, along_y),
-        (ST_C, st_c, core, [sibling]),
-        (ST_L, st_l, zl, along_l),
-        (ST_P, st_p, zh, [partner]),
-    )
+    stages = ((ST_X, st_x, x, along_x), (ST_Y, st_y, y, along_y), (ST_L, st_l, zl, along_l), (ST_P, st_p, zh, [partner]))
+    to_native = copy(ST_C, st_c.at[0], st_c.at[1], sibling)
+    to_foreign = copy(ST_C + 1, st_c.at[0], st_c.at[1], sibling)
+
+    def own_sums():
+        return (acc[:, :, :128] + acc[:, :, 128:]).reshape(24, 128)
 
     def stage_copies(base, buffer, mine, line):
         return [copy(base + i, buffer.at[mine], buffer.at[mine], other) for i, other in enumerate(line)]
@@ -297,14 +296,7 @@
         buffer, count = stages[stage][1], len(stages[stage][3]) + 1
         return functools.reduce(lambda a, b: a + b, [buffer[i] for i in range(count)])
 
-    def sums_first():
-        sums_start(0, (acc[:, :, :128] + acc[:, :, 128:]).reshape(24, 128))
-
-    def sums_next(stage):
-        sums_start(stage, sums_finish(stage - 1))
-
-    def sums_last():
-        totals = sums_finish(len(stages) - 1)
+    def write_totals(totals):
         for k, factor in enumerate((1.0, scale[:, :1], 1.0)):
             total = jnp.sum(jnp.sum(totals[8 * k : 8 * k + 8], axis=0, keepdims=True), axis=1, keepdims=True)
             out_totals[k : k + 1, :] = jnp.broadcast_to(factor * total / pairs, (1, 128))
@@ -316,6 +308,15 @@
             for step in steps:
                 reduce(t, h, step).wait_send()
 
+    def start_both(t, step):
+        reduce(t, A, step).start()
+        reduce(t, B, step).start()
+
+    def wait_sent(t, steps):
+        for step in steps:
+            reduce(t, A, step).wait_send()
+            reduce(t, B, step).wait_send()
+
     @pl.when(native)
     def _():
         for t in (TXT, IMG):
@@ -325,47 +326,52 @@
         for t in (TXT, IMG):
             pass_on(t, A)
             pass_on(t, B)
-            pass_last(t, A)
-            pass_last(t, B)
         own_logits(A, 0, tiles)
         own_logits(B, 0, tiles)
         from_core(TXT, A)
         from_core(TXT, B)
         own_logits(A, tiles, 2 * tiles)
         same_pairs(A)
-        image_terms(A)
         own_logits(B, tiles, 2 * tiles)
         same_pairs(B)
+        image_terms(A)
         image_terms(B)
-        sums_first()
-        add_relayed(IMG, A)
-        add_relayed(IMG, B)
         from_core(IMG, A)
         other_logits(A)
-        sums_next(1)
+        to_native.wait_recv()
+        sums_start(0, own_sums() + st_c[1])
         from_core(IMG, B)
         other_logits(B)
+        sums_start(1, sums_finish(0))
         text_terms(A)
         text_terms(B)
-        sums_next(2)
-        for h in (A, B):
-            finish(IMG, h)
-            local_out(IMG, h).start()
-        pl.semaphore_wait(turn, 1)
-        text_start(A)
-        text_start(B)
-        sums_next(3)
-        add_relayed(TXT, A)
-        add_relayed(TXT, B)
-        sums_next(4)
-        for h in (A, B):
-            finish(TXT, h)
-            local_out(TXT, h).start()
-        sums_last()
-        for t in (IMG, TXT):
+        sums_start(2, sums_finish(1))
+        sums_start(3, sums_finish(2))
+        totals = sums_finish(3)
+        st_c[0] = totals
+        to_foreign.start()
+        write_totals(totals)
+        for t in (TXT, IMG):
+            pl.semaphore_wait(turn.at[t], 1)
+            start_both(t, 0)
+        for t in (TXT, IMG):
+            wait_sent(t, (0,))
+            start_both(t, 1)
+        for t in (TXT, IMG):
+            add_relayed(t, A)
+            add_relayed(t, B)
+        for t in (TXT, IMG):
+            for h in (A, B):
+                finish(t, h)
+                local_out(t, h).start()
+        to_foreign.wait_send()
+        for stage in stages:
+            for each in stage_copies(*stage):
+                each.wait_send()
+        for t in (TXT, IMG):
+            wait_sent(t, (1, 2))
             for h in (A, B):
                 local_out(t, h).wait()
-        wait_sent(TXT, (2,))
 
     @pl.when(jnp.logical_not(native))
     def _():
@@ -376,60 +382,66 @@
         send_half(TXT, A)
         z_in(TXT, B).wait_send()
         z_in(IMG, A).start()
-        pass_on(TXT, A)
         z_in(TXT, B).wait_recv()
         send_half(TXT, B)
         z_in(IMG, A).wait_send()
         z_in(IMG, B).start()
-        pass_last(TXT, A)
+        pass_on(TXT, A)
         z_in(IMG, A).wait_recv()
         send_half(IMG, A)
         pass_on(TXT, B)
-        z_in(IMG, B).wait_recv()
-        send_half(IMG, B)
-        pass_on(IMG, A)
-        pass_last(TXT, B)
         from_core(IMG, A)
         from_core(IMG, B)
         other_logits(A)
+        z_in(IMG, B).wait_recv()
+        send_half(IMG, B)
         other_logits(B)
         from_core(TXT, A)
         from_core(TXT, B)
-        pass_last(IMG, A)
-        own_logits(A, 0, tiles)
+        pass_on(IMG, A)
+        own_logits(A, 0, 2 * tiles)
+        same_pairs(A)
+        image_terms(A)
+        reduce(IMG, A, 0).start()
+        reduce(IMG, A, 1).start()
+        text_early(A)
+        text_early(B)
         pass_on(IMG, B)
-        own_logits(A, tiles, 2 * tiles)
-        same_pairs(A)
-        pass_last(IMG, B)
-        image_terms(A)
         own_logits(B, 0, 2 * tiles)
         same_pairs(B)
-        text_terms(A)
-        text_start(A)
-        text_terms(B)
-        text_start(B)
-        sums_first()
+        st_c[0] = own_sums()
+        to_native.start()
+        text_late(A)
+        reduce(TXT, A, 0).start()
+        text_late(B)
+        reduce(TXT, B, 0).start()
         add_relayed(IMG, A)
         image_terms(B)
+        reduce(IMG, B, 0).start()
+        reduce(IMG, B, 1).start()
+        wait_sent(TXT, (0,))
+        start_both(TXT, 1)
         add_relayed(TXT, A)
         add_relayed(TXT, B)
-        sums_next(1)
-        add_relayed(IMG, B)
         finish(IMG, A)
         z_out(IMG, A).start()
-        sums_next(2)
+        add_relayed(IMG, B)
         wait_sent(TXT, (2,))
-        pl.semaphore_signal(turn, inc=1, device_id=sibling, device_id_type=MESH)
+        pl.semaphore_signal(turn.at[TXT], inc=1, device_id=sibling, device_id_type=MESH)
         finish(TXT, A)
         z_out(TXT, A).start()
         finish(TXT, B)
         z_out(TXT, B).start()
+        wait_sent(IMG, (2,))
+        pl.semaphore_signal(turn.at[IMG], inc=1, device_id=sibling, device_id_type=MESH)
         finish(IMG, B)
         z_out(IMG, B).start()
-        sums_next(3)
-        sums_next(4)
-        sums_last()
+        to_foreign.wait_recv()
+        write_totals(st_c[1])
+        to_native.wait_send()
         z_in(IMG, B).wait_send()
+        wait_sent(TXT, (1,))
+        wait_sent(IMG, (0, 1))
         for t in (IMG, TXT):
             for h in (A, B):
                 z_out(t, h).wait()
@@ -438,14 +450,9 @@
         for h in (A, B):
             gather(t, h, 0).wait_send()
             gather(t, h, 1).wait_send()
-            relay(t, h).wait_send()
+            across(t, h).wait_send()
             for index in range(SIDE):
                 to_core(t, h, index).wait_send()
-    wait_sent(TXT, (0, 1))
-    wait_sent(IMG, (0, 1, 2))
-    for stage in stages:
-        for each in stage_copies(*stage):
-            each.wait_send()
 
 
 def per_device(image_embed, text_embed, log_logit_scale, logit_bias):
@@ -488,7 +495,7 @@
             pltpu.SemaphoreType.DMA((COPIES,)),
             pltpu.SemaphoreType.DMA((COPIES,)),
             pltpu.SemaphoreType.DMA((8,)),
-            pltpu.SemaphoreType.REGULAR,
+            pltpu.SemaphoreType.REGULAR((2,)),
         ],
         name="contrastive_step",
         compiler_params=pltpu.CompilerParams(

time: 100 us -> 87.7 us (0.88)
  the two profiles are of different devices: /device:TPU:1 before, /device:TPU:33 now
where the time goes in v4:
time: 87.7 us; the launch traced here: 87.5 us
  Pallas kernels  81.7 us (93%)
  local copies, waits for them, and re-layouts  3.87 us (4%)
  between operations  1.93 us (2%)
    pallas_call x1, Pallas kernels, per_device(): pl.pallas_call(functools.partial(kernel, pairs), out_shape=(like, like, j...  81.7 us
    unnamed x4, local copies, waits for them, and re-layouts  2.57 us

profile of v4, /device:TPU:33, one launch (start us, length us, event | category | flops | bytes accessed | tf_op | source)
XLA Modules:
  0.0 87.5 jit_solution(6044122678419095991)
XLA Ops:
  1.9 81.7 %contrastive_step.1 = (bf16[192,1024]{1,0:T(8,128)(2,1)}, bf16[192,1024]{1,0:T(8,128)(2,1)}, f32[8,128]{1,0:T(8,128)}) custom-call(f32[1]{0:T(128)S(6)} %copy.11.log_scale_any, f32[1]{0:T(128)S(6)} %copy.12.bias_any, bf16[192,1024]{1,0:T(8,128)(2,1)} %img_ref.1, bf16[192,1024]{1,0:T(8,128)(2,1)} %txt_ref.1), custom_call_target="tpu_custom_call" | custom-call | tf_op jit(solution)/shard_map/contrastive_step/pallas_call | solution.py:466
  83.6 1.3 %fusion = (f32[1,1]{1,0:T(1,128)}, f32[1,1]{1,0:T(1,128)}, f32[1,1]{1,0:T(1,128)}) fusion(f32[8,128]{1,0:T(8,128)} %get-tuple-element.10), kind=kLoop, calls=%fused_computation | loop fusion | bytes 24 | tf_op jit(solution)/shard_map/slice | solution.py:505
  84.9 0.0 copy-start
  84.9 1.8 %copy.13 = bf16[192,1024]{1,0:T(8,128)(2,1)} copy(bf16[192,1024]{1,0:T(8,128)(2,1)} %get-tuple-element.19) | data formatting | bytes 786432
  86.8 0.0 copy-done
  86.8 0.7 copy.14
Async XLA Ops:
  84.9 1.8 %copy-start = (bf16[192,1024]{1,0:T(8,128)(2,1)S(1)}, bf16[192,1024]{1,0:T(8,128)(2,1)}, u32[]{:S(2)}) copy-start(bf16[192,1024]{1,0:T(8,128)(2,1)} %get-tuple-element.20) | copy-start | bytes 1179652

commit v5 on v4

--- a/solution.py
+++ b/solution.py
@@ -25,7 +25,7 @@
 
 def kernel(
     pairs, log_scale_any, bias_any, img_ref, txt_ref,
-    out_img, out_txt, out_totals,
+    out_grads, out_totals,
     raw, inverses, texts, images, coef_own, coef_other, cos_even, cos_odd,
     grad_txt, grad_img, recv_txt, recv_img, relay_txt, relay_img,
     final, acc, st_x, st_y, st_c, st_l, st_p, log_scale_ref, bias_ref, send_sem, recv_sem, local_sem, turn,
@@ -54,7 +54,7 @@
     left = (along_x[2], along_y[2])
     sibling = device(other_core=True)
     partner = device(other_core=True, other_plane=True)
-    inputs, outputs = (txt_ref, img_ref), (out_txt, out_img)
+    inputs, outputs = (txt_ref, img_ref), (out_grads.at[TXT], out_grads.at[IMG])
     units, grads = (texts, images), (grad_txt, grad_img)
     recvs, relays = (recv_txt, recv_img), (relay_txt, relay_img)
 
@@ -402,21 +402,22 @@
         own_logits(A, 0, 2 * tiles)
         same_pairs(A)
         image_terms(A)
-        reduce(IMG, A, 0).start()
-        reduce(IMG, A, 1).start()
         text_early(A)
         text_early(B)
         pass_on(IMG, B)
-        own_logits(B, 0, 2 * tiles)
+        reduce(IMG, A, 0).start()
+        reduce(IMG, A, 1).start()
+        own_logits(B, 0, tiles)
         same_pairs(B)
-        st_c[0] = own_sums()
-        to_native.start()
         text_late(A)
         reduce(TXT, A, 0).start()
         text_late(B)
         reduce(TXT, B, 0).start()
+        own_logits(B, tiles, 2 * tiles)
+        st_c[0] = own_sums()
+        to_native.start()
+        image_terms(B)
         add_relayed(IMG, A)
-        image_terms(B)
         reduce(IMG, B, 0).start()
         reduce(IMG, B, 1).start()
         wait_sent(TXT, (0,))
@@ -461,13 +462,13 @@
     block = share // 2
     pairs = rows * lax.axis_size("blk") * lax.axis_size("dp")
     hbm, vmem = pl.BlockSpec(memory_space=pltpu.HBM), pl.BlockSpec(memory_space=pltpu.VMEM)
-    like = jax.ShapeDtypeStruct((rows, width), jnp.bfloat16)
+    like = jax.ShapeDtypeStruct((2, rows, width), jnp.bfloat16)
     bf16, f32 = jnp.bfloat16, jnp.float32
-    image_gradient, text_gradient, totals = pl.pallas_call(
+    gradients, totals = pl.pallas_call(
         functools.partial(kernel, pairs),
-        out_shape=(like, like, jax.ShapeDtypeStruct((8, 128), f32)),
+        out_shape=(like, jax.ShapeDtypeStruct((8, 128), f32)),
         in_specs=[hbm, hbm, hbm, hbm],
-        out_specs=(hbm, hbm, vmem),
+        out_specs=(hbm, vmem),
         scratch_shapes=[
             pltpu.VMEM((2, rows, width), bf16),
             pltpu.VMEM((2, rows, 128), f32),
@@ -503,7 +504,7 @@
         ),
     )(log_logit_scale, logit_bias, image_embed, text_embed)
     loss, scale_gradient, bias_gradient = totals[0, :1], totals[1, :1], totals[2, :1]
-    return image_gradient, text_gradient, scale_gradient, bias_gradient, loss
+    return gradients[IMG], gradients[TXT], scale_gradient, bias_gradient, loss
 
 
 def solution(mesh):

time: 87.7 us -> 85.4 us (0.974)
  Pallas kernels: 81.7 us -> 79.3 us
    unnamed x4 -> x0, local copies, waits for them, and re-layouts: 2.57 us -> none
    pallas_call x1, Pallas kernels: 81.7 us -> 79.3 us  [per_device(): pl.pallas_call(functools.partial(kernel, pairs), out_shape=(like, jax.Sha...]
    squeeze x0 -> x1, local copies, waits for them, and re-layouts: none -> 2.04 us  [per_device(): return (gradients[IMG], gradients[TXT], scale_gradient, bias_gradient, loss)]
where the time goes in v5:
time: 85.4 us; the launch traced here: 84.6 us
  Pallas kernels  79.3 us (93%)
  local copies, waits for them, and re-layouts  3.35 us (4%)
  between operations  1.93 us (2%)
    pallas_call x1, Pallas kernels, per_device(): pl.pallas_call(functools.partial(kernel, pairs), out_shape=(like, jax.Sha...  79.3 us
    squeeze x1, local copies, waits for them, and re-layouts, per_device(): return (gradients[IMG], gradients[TXT], scale_gradient, bias_gradient, loss)  2.04 us

profile of v5, /device:TPU:33, one launch (start us, length us, event | category | flops | bytes accessed | tf_op | source)
XLA Modules:
  0.0 84.6 jit_solution(17690638104225656621)
XLA Ops:
  1.9 79.3 %contrastive_step.1 = (bf16[2,192,1024]{2,1,0:T(8,128)(2,1)}, f32[8,128]{1,0:T(8,128)}) custom-call(f32[1]{0:T(128)S(6)} %copy.9.log_scale_any, f32[1]{0:T(128)S(6)} %copy.10.bias_any, bf16[192,1024]{1,0:T(8,128)(2,1)} %img_ref.1, bf16[192,1024]{1,0:T(8,128)(2,1)} %txt_ref.1), custom_call_target="tpu_custom_call" | custom-call | tf_op jit(solution)/shard_map/contrastive_step/pallas_call | solution.py:467
  81.3 1.3 %fusion = (f32[1,1]{1,0:T(1,128)}, f32[1,1]{1,0:T(1,128)}, f32[1,1]{1,0:T(1,128)}) fusion(f32[8,128]{1,0:T(8,128)} %get-tuple-element.8), kind=kLoop, calls=%fused_computation.2 | loop fusion | bytes 24 | tf_op jit(solution)/shard_map/slice | solution.py:506
  82.6 2.0 %slice_bitcast_fusion = (bf16[192,1024]{1,0:T(8,128)(2,1)}, bf16[192,1024]{1,0:T(8,128)(2,1)}) fusion(bf16[2,192,1024]{2,1,0:T(8,128)(2,1)} %get-tuple-element.7), kind=kLoop, calls=%fused_computation | loop fusion | bytes 1572864 | tf_op jit(solution)/shard_map/squeeze | solution.py:507

commit v6 on v5

--- a/solution.py
+++ b/solution.py
@@ -24,11 +24,11 @@
 
 
 def kernel(
-    pairs, log_scale_any, bias_any, img_ref, txt_ref,
+    pairs, log_scale_ref, bias_ref, img_ref, txt_ref,
     out_grads, out_totals,
     raw, inverses, texts, images, coef_own, coef_other, cos_even, cos_odd,
     grad_txt, grad_img, recv_txt, recv_img, relay_txt, relay_img,
-    final, acc, st_x, st_y, st_c, st_l, st_p, log_scale_ref, bias_ref, send_sem, recv_sem, local_sem, turn,
+    final, acc, st_x, st_y, st_c, st_l, st_p, send_sem, recv_sem, local_sem, turn,
 ):
     rows, width = img_ref.shape
     part = rows // 2
@@ -108,13 +108,6 @@
     def local_out(t, h):
         return pltpu.make_async_copy(final.at[t, half(h)], outputs[t].at[half(h)], local_sem.at[2 + 2 * t + h])
 
-    scalar_copies = [
-        pltpu.make_async_copy(src, dst, local_sem.at[6 + i])
-        for i, (src, dst) in enumerate(((log_scale_any, log_scale_ref), (bias_any, bias_ref)))
-    ]
-    for each in scalar_copies:
-        each.start()
-
     @pl.when(native)
     def _():
         local_in(TXT).start()
@@ -126,12 +119,11 @@
         pl.semaphore_signal(barrier, inc=1, device_id=other, device_id_type=MESH)
     pl.semaphore_wait(barrier, len(everyone))
 
-    for each in scalar_copies:
-        each.wait()
-    log_scale = jnp.full((1, TILE), log_scale_ref[0], jnp.float32)
+    log_scale = jnp.broadcast_to(log_scale_ref[...], (1, TILE))
     scale = jnp.exp(log_scale)
     scale2 = scale * LOG2E
-    bias2 = jnp.full((1, TILE), bias_ref[0], jnp.float32) * LOG2E
+    bias = jnp.broadcast_to(bias_ref[...], (1, TILE))
+    bias2 = bias * LOG2E
     acc[...] = jnp.zeros_like(acc)
 
     def normalize(t, h):
@@ -226,7 +218,7 @@
         inverse = 1.0 / more
         coef = grown * inverse
         coef_own[at_rows, at_cols] = jnp.where(same, -inverse, coef).astype(jnp.bfloat16)
-        logit = scale[:, :lanes] * cosine + bias_ref[0]
+        logit = scale[:, :lanes] * cosine + bias[:, :lanes]
         change = jnp.where(same, -inverse - coef, 0.0)
         fold = (part // 8, 8, lanes)
         acc[0, :, :lanes] += jnp.sum(jnp.where(same, -logit, 0.0).reshape(fold), axis=0)
@@ -264,12 +256,12 @@
     def finish(t, h):
         reduce(t, h, 1).wait_recv()
         reduce(t, h, 2).wait_recv()
-        for i in range(part // 16):
-            at = pl.ds(h * part + i * 16, 16)
+        for i in range(part // 32):
+            at = pl.ds(h * part + i * 32, 32)
             inverse = inverses[t, at, :1]
             unit = raw[t, at, :].astype(jnp.float32) * inverse
             scaled = scale[:, :1] * (
-                grads[t][pl.ds(h * block + i * 16, 16), :] + recvs[t][0, at, :] + recvs[t][1, at, :]
+                grads[t][pl.ds(h * block + i * 32, 32), :] + recvs[t][0, at, :] + recvs[t][1, at, :]
             )
             along = jnp.sum(unit * scaled, axis=1, keepdims=True)
             final[t, at, :] = ((scaled - unit * along) * inverse).astype(jnp.bfloat16)
@@ -351,16 +343,18 @@
         st_c[0] = totals
         to_foreign.start()
         write_totals(totals)
-        for t in (TXT, IMG):
-            pl.semaphore_wait(turn.at[t], 1)
-            start_both(t, 0)
-        for t in (TXT, IMG):
-            wait_sent(t, (0,))
-            start_both(t, 1)
-        for t in (TXT, IMG):
+        pl.semaphore_wait(turn.at[IMG], 1)
+        start_both(IMG, 0)
+        pl.semaphore_wait(turn.at[TXT], 1)
+        start_both(TXT, 0)
+        wait_sent(IMG, (0,))
+        start_both(IMG, 1)
+        wait_sent(TXT, (0,))
+        start_both(TXT, 1)
+        for t in (IMG, TXT):
             add_relayed(t, A)
             add_relayed(t, B)
-        for t in (TXT, IMG):
+        for t in (IMG, TXT):
             for h in (A, B):
                 finish(t, h)
                 local_out(t, h).start()
@@ -424,9 +418,10 @@
         start_both(TXT, 1)
         add_relayed(TXT, A)
         add_relayed(TXT, B)
+        add_relayed(IMG, B)
+        pl.semaphore_signal(turn.at[IMG], inc=1, device_id=sibling, device_id_type=MESH)
         finish(IMG, A)
         z_out(IMG, A).start()
-        add_relayed(IMG, B)
         wait_sent(TXT, (2,))
         pl.semaphore_signal(turn.at[TXT], inc=1, device_id=sibling, device_id_type=MESH)
         finish(TXT, A)
@@ -434,7 +429,6 @@
         finish(TXT, B)
         z_out(TXT, B).start()
         wait_sent(IMG, (2,))
-        pl.semaphore_signal(turn.at[IMG], inc=1, device_id=sibling, device_id_type=MESH)
         finish(IMG, B)
         z_out(IMG, B).start()
         to_foreign.wait_recv()
@@ -467,7 +461,7 @@
     gradients, totals = pl.pallas_call(
         functools.partial(kernel, pairs),
         out_shape=(like, jax.ShapeDtypeStruct((8, 128), f32)),
-        in_specs=[hbm, hbm, hbm, hbm],
+        in_specs=[vmem, vmem, hbm, hbm],
         out_specs=(hbm, vmem),
         scratch_shapes=[
             pltpu.VMEM((2, rows, width), bf16),
@@ -491,18 +485,16 @@
             pltpu.VMEM((2, 24, 128), f32),
             pltpu.VMEM((4, 24, 128), f32),
             pltpu.VMEM((2, 24, 128), f32),
-            pltpu.SMEM((1,), f32),
-            pltpu.SMEM((1,), f32),
             pltpu.SemaphoreType.DMA((COPIES,)),
             pltpu.SemaphoreType.DMA((COPIES,)),
-            pltpu.SemaphoreType.DMA((8,)),
+            pltpu.SemaphoreType.DMA((6,)),
             pltpu.SemaphoreType.REGULAR((2,)),
         ],
         name="contrastive_step",
         compiler_params=pltpu.CompilerParams(
             collective_id=0, has_side_effects=True, vmem_limit_bytes=62 * 2**20
         ),
-    )(log_logit_scale, logit_bias, image_embed, text_embed)
+    )(log_logit_scale.reshape(1, 1), logit_bias.reshape(1, 1), image_embed, text_embed)
     loss, scale_gradient, bias_gradient = totals[0, :1], totals[1, :1], totals[2, :1]
     return gradients[IMG], gradients[TXT], scale_gradient, bias_gradient, loss
 

time: 85.4 us -> 85.1 us (level)
  no operation moved by 1% of the time
where the time goes in v6:
time: 85.1 us; the launch traced here: 84.4 us
  Pallas kernels  79.1 us (93%)
  local copies, waits for them, and re-layouts  3.35 us (4%)
  between operations  1.93 us (2%)
    pallas_call x1, Pallas kernels, per_device(): pl.pallas_call(functools.partial(kernel, pairs), out_shape=(like, jax.Sha...  79.1 us
    squeeze x1, local copies, waits for them, and re-layouts, per_device(): return (gradients[IMG], gradients[TXT], scale_gradient, bias_gradient, loss)  2.04 us

profile of v6, /device:TPU:33, one launch (start us, length us, event | category | flops | bytes accessed | tf_op | source)
XLA Modules:
  0.0 84.4 jit_solution(12316122334133277661)
XLA Ops:
  1.9 79.1 %contrastive_step.1 = (bf16[2,192,1024]{2,1,0:T(8,128)(2,1)}, f32[8,128]{1,0:T(8,128)}) custom-call(f32[1,1]{1,0:T(1,128)} %bitcast.9.log_scale_ref, f32[1,1]{1,0:T(1,128)} %bitcast.10.bias_ref, bf16[192,1024]{1,0:T(8,128)(2,1)} %img_ref.1, bf16[192,1024]{1,0:T(8,128)(2,1)} %txt_ref.1), custom_call_target="tpu_custom_call" | custom-call | tf_op jit(solution)/shard_map/contrastive_step/pallas_call | solution.py:461
  81.1 1.3 %fusion = (f32[1,1]{1,0:T(1,128)}, f32[1,1]{1,0:T(1,128)}, f32[1,1]{1,0:T(1,128)}) fusion(f32[8,128]{1,0:T(8,128)} %get-tuple-element.8), kind=kLoop, calls=%fused_computation.2 | loop fusion | bytes 24 | tf_op jit(solution)/shard_map/slice | solution.py:498
  82.4 2.0 %slice_bitcast_fusion = (bf16[192,1024]{1,0:T(8,128)(2,1)}, bf16[192,1024]{1,0:T(8,128)(2,1)}) fusion(bf16[2,192,1024]{2,1,0:T(8,128)(2,1)} %get-tuple-element.7), kind=kLoop, calls=%fused_computation | loop fusion | bytes 1572864 | tf_op jit(solution)/shard_map/squeeze | solution.py:499

commit v7 on v6

--- a/solution.py
+++ b/solution.py
@@ -114,10 +114,9 @@
         local_in(IMG).start()
 
     barrier = pltpu.get_barrier_semaphore()
-    everyone = along_x + along_y + along_l + [sibling, partner]
+    everyone = [partner] + along_l + along_x + along_y + [sibling]
     for other in everyone:
         pl.semaphore_signal(barrier, inc=1, device_id=other, device_id_type=MESH)
-    pl.semaphore_wait(barrier, len(everyone))
 
     log_scale = jnp.broadcast_to(log_scale_ref[...], (1, TILE))
     scale = jnp.exp(log_scale)
@@ -125,6 +124,7 @@
     bias = jnp.broadcast_to(bias_ref[...], (1, TILE))
     bias2 = bias * LOG2E
     acc[...] = jnp.zeros_like(acc)
+    pl.semaphore_wait(barrier, len(everyone))
 
     def normalize(t, h):
         for i in range(part // 32):

time: 85.1 us -> 85 us (level)
  no operation moved by 1% of the time
where the time goes in v7:
time: 85 us; the launch traced here: 84.2 us
  Pallas kernels  78.9 us (93%)
  local copies, waits for them, and re-layouts  3.35 us (4%)
  between operations  1.93 us (2%)
    pallas_call x1, Pallas kernels, per_device(): pl.pallas_call(functools.partial(kernel, pairs), out_shape=(like, jax.Sha...  78.9 us
    squeeze x1, local copies, waits for them, and re-layouts, per_device(): return (gradients[IMG], gradients[TXT], scale_gradient, bias_gradient, loss)  2.04 us

profile of v7, /device:TPU:33, one launch (start us, length us, event | category | flops | bytes accessed | tf_op | source)
XLA Modules:
  0.0 84.2 jit_solution(7438574189563380236)
XLA Ops:
  1.9 78.9 %contrastive_step.1 = (bf16[2,192,1024]{2,1,0:T(8,128)(2,1)}, f32[8,128]{1,0:T(8,128)}) custom-call(f32[1,1]{1,0:T(1,128)} %bitcast.9.log_scale_ref, f32[1,1]{1,0:T(1,128)} %bitcast.10.bias_ref, bf16[192,1024]{1,0:T(8,128)(2,1)} %img_ref.1, bf16[192,1024]{1,0:T(8,128)(2,1)} %txt_ref.1), custom_call_target="tpu_custom_call" | custom-call | tf_op jit(solution)/shard_map/contrastive_step/pallas_call | solution.py:461
  80.8 1.3 %fusion = (f32[1,1]{1,0:T(1,128)}, f32[1,1]{1,0:T(1,128)}, f32[1,1]{1,0:T(1,128)}) fusion(f32[8,128]{1,0:T(8,128)} %get-tuple-element.8), kind=kLoop, calls=%fused_computation.2 | loop fusion | bytes 24 | tf_op jit(solution)/shard_map/slice | solution.py:498
  82.1 2.0 %slice_bitcast_fusion = (bf16[192,1024]{1,0:T(8,128)(2,1)}, bf16[192,1024]{1,0:T(8,128)(2,1)}) fusion(bf16[2,192,1024]{2,1,0:T(8,128)(2,1)} %get-tuple-element.7), kind=kLoop, calls=%fused_computation | loop fusion | bytes 1572864 | tf_op jit(solution)/shard_map/squeeze | solution.py:499
